TPU v7x, 32 devices: a whole 2x2x4 slice. The times are simulated.
32 devices in a mesh: groups: 2 (over y), gx: 4 (over z), gy: 4 (over x, core).
Axes of the slice: x: 2, y: 2, z: 4, core: 2. Of those that a mesh axis runs over, the one named last changes fastest.
Arguments:
- residual: bfloat16 [64, 8192], P(('groups', 'gx'), 'gy'), parts along dimension 0, may hold values from -50 to 50
- norm_gain: bfloat16 [8192], P('gy'), may hold values from 0.5 to 2
- qkv_weight: bfloat16 [8192, 4608], P('gy', 'gx'), may hold values from -0.0625 to 0.0625
- out_weight: bfloat16 [4096, 8192], P('gx', 'gy'), may hold values from -0.375 to 0.375
- gate_weight: bfloat16 [8192, 16384], P('gy', 'gx'), may hold values from -0.0625 to 0.0625
- up_weight: bfloat16 [8192, 16384], P('gy', 'gx'), may hold values from -0.0625 to 0.0625
- down_weight: bfloat16 [16384, 8192], P('gx', 'gy'), may hold values from -0.046875 to 0.046875
- cache_keys: bfloat16 [64, 512, 256], P(('groups', 'gx', 'gy')), parts along dimension 0, may hold values from -150 to 150
- cache_values: bfloat16 [64, 512, 256], P(('groups', 'gx', 'gy')), parts along dimension 0, may hold values from -6 to 6
- lengths: int32 [64], P(('groups', 'gx', 'gy')), parts along dimension 0, may hold values from 1 to 512, as said below
- positions: int32 [64], P(('groups', 'gx', 'gy')), parts along dimension 0, may hold values from 0 to 2047
Outputs:
- update: bfloat16 [64, 8192], P(('groups', 'gx'), 'gy'), parts along dimension 0
There are 2 independent parts, one for each index of `groups`. A program takes and returns all parts, laid end to end along the dimension named above; an argument that names none is the same for every part. Nothing has to cross between parts.
Inputs may be any that keep to these rules, and one draw needn't show every extreme that they name: `lengths`: at least one row has exactly 512 valid slots.
All inputs are finite; a program needn't handle non-finite values.
Results may differ from a plain program's by a relative error of at most 0.012.
Values may be sent and summed in bfloat16 or wider, within the bound.
A program may use at most 128 MiB of HBM per device.

v0:
```python
import jax
import jax.numpy as jnp
from jax import lax
from jax.sharding import PartitionSpec as P

D = 8192


def angles(token_positions, head_width):
    half_width = head_width // 2
    frequency = jnp.exp(
        jnp.arange(half_width, dtype=jnp.float32) * (-2.0 * jnp.log(10000.0) / head_width)
    )
    return token_positions.astype(jnp.float32)[:, None] * frequency[None, :]


def rotary(vectors, turn):
    half_width = vectors.shape[-1] // 2
    first_half = vectors[..., :half_width]
    second_half = vectors[..., half_width:]
    cosine = jnp.cos(turn)
    sine_part = jnp.sin(turn)
    return jnp.concatenate(
        [
            first_half * cosine - second_half * sine_part,
            first_half * sine_part + second_half * cosine,
        ],
        axis=-1,
    )


def attend(joined, cached_keys, cached_values, valid_lengths, token_positions):
    row_count = joined.shape[0]
    head_width = cached_keys.shape[2]
    query_width = joined.shape[1] - 2 * head_width
    head_count = query_width // head_width
    queries = joined[:, :query_width].astype(jnp.float32).reshape(row_count, head_count, head_width)
    new_key = joined[:, query_width : query_width + head_width].astype(jnp.float32)
    new_value = joined[:, query_width + head_width :].astype(jnp.float32)
    turn = angles(token_positions, head_width)
    rotated_queries = rotary(queries, turn[:, None, :]).astype(jnp.bfloat16)
    rotated_key = rotary(new_key, turn).astype(jnp.bfloat16)
    score_scale = head_width ** (-0.5)
    scores = (
        jnp.einsum("rhd,rcd->rhc", rotated_queries, cached_keys, preferred_element_type=jnp.float32)
        * score_scale
    )
    visible = (
        jnp.arange(cached_keys.shape[1], dtype=jnp.int32)[None, None, :]
        < valid_lengths[:, None, None]
    )
    scores = jnp.where(visible, scores, -jnp.inf)
    own_score = (
        jnp.einsum("rhd,rd->rh", rotated_queries, rotated_key, preferred_element_type=jnp.float32)
        * score_scale
    )
    top_score = jnp.maximum(jnp.max(scores, axis=2), own_score)
    shifted = jnp.exp(scores - top_score[:, :, None])
    own_shifted = jnp.exp(own_score - top_score)
    denominator = jnp.sum(shifted, axis=2) + own_shifted
    softmax_weights = (shifted / denominator[:, :, None]).astype(jnp.bfloat16)
    own_weight = (own_shifted / denominator).astype(jnp.bfloat16)
    mixed = jnp.einsum(
        "rhc,rcd->rhd", softmax_weights, cached_values, preferred_element_type=jnp.float32
    )
    mixed = mixed + own_weight.astype(jnp.float32)[:, :, None] * new_value[:, None, :]
    return mixed.reshape(row_count, query_width).astype(jnp.bfloat16)


def shards(
    residual,
    norm_gain,
    qkv_weight,
    out_weight,
    gate_weight,
    up_weight,
    down_weight,
    cache_keys,
    cache_values,
    lengths,
    positions,
):
    gain_wide = norm_gain.astype(jnp.float32)
    widened = residual.astype(jnp.float32)
    totals = lax.psum(jnp.sum(widened * widened, axis=1), "gy")
    scaled_rows = (widened * lax.rsqrt(totals / D + 1e-06)[:, None] * gain_wide).astype(
        jnp.bfloat16
    )
    normed = lax.all_gather(scaled_rows, "gx", axis=0, tiled=True)
    qkv_part = jnp.dot(normed, qkv_weight, preferred_element_type=jnp.float32)
    gate_part = jnp.dot(normed, gate_weight, preferred_element_type=jnp.float32)
    up_part = jnp.dot(normed, up_weight, preferred_element_type=jnp.float32)
    swapped = lax.all_to_all(qkv_part, "gx", split_axis=0, concat_axis=1, tiled=True)
    rows_qkv = lax.psum_scatter(swapped, "gy", scatter_dimension=0, tiled=True).astype(jnp.bfloat16)
    attended = attend(rows_qkv, cache_keys, cache_values, lengths, positions)
    grouped = lax.all_gather(attended, "gy", axis=0, tiled=True)
    heads_out = lax.all_to_all(grouped, "gx", split_axis=1, concat_axis=0, tiled=True)
    gate_sum, up_sum = lax.psum((gate_part, up_part), "gy")
    hidden = (jax.nn.silu(gate_sum) * up_sum).astype(jnp.bfloat16)
    block_term = jnp.dot(heads_out, out_weight, preferred_element_type=jnp.float32)
    return lax.psum_scatter(
        (block_term + jnp.dot(hidden, down_weight, preferred_element_type=jnp.float32)).astype(
            jnp.bfloat16
        ),
        "gx",
        scatter_dimension=0,
        tiled=True,
    )


def solution(mesh):
    in_specs = (
        P(("groups", "gx"), "gy"),
        P("gy"),
        P("gy", "gx"),
        P("gx", "gy"),
        P("gy", "gx"),
        P("gy", "gx"),
        P("gx", "gy"),
        P(("groups", "gx", "gy"), None, None),
        P(("groups", "gx", "gy"), None, None),
        P(("groups", "gx", "gy")),
        P(("groups", "gx", "gy")),
    )
    out_specs = P(("groups", "gx"), "gy")
    return jax.shard_map(shards, mesh=mesh, in_specs=in_specs, out_specs=out_specs, check_vma=False)
```

profile of v0, /device:TPU:0, one launch (start us, length us, event | category | flops | bytes accessed | tf_op | source)
XLA Modules:
  0.0 128.5 jit_solution(14645805836541470734)
XLA Ops:
  6.5 0.9 fusion.4
  7.5 8.3 %psum.21 = f32[8]{0:T(128)S(1)} all-reduce(f32[8]{0:T(128)S(1)} %fusion.4), channel_id=1, replica_groups=mesh['groups'=2,'gx'=4,'gy'=4] {'gy'}, use_global_device_ids=true, to_apply=%region_1.0 | all-reduce | flops 8 | bytes 64 | tf_op jit(solution)/shard_map/psum | solution.py:85
  15.8 0.7 convert_element_type.46
  16.5 0.8 fusion.6
  17.4 13.6 %all_gather.6 = bf16[32,2048]{1,0:T(8,128)(2,1)S(1)} all-gather(bf16[8,2048]{1,0:T(8,128)(2,1)S(1)} %fusion.6), channel_id=1, replica_groups=mesh['groups'=2,'gx'=4,'gy'=4] {'gx'}, dimensions={0}, use_global_device_ids=true | all-gather | bytes 163840 | tf_op jit(solution)/shard_map/all_gather | solution.py:89
  31.0 3.9 %convolution_bitcast_fusion = f32[4,8,1152]{2,1,0:T(8,128)} fusion(bf16[32,2048]{1,0:T(8,128)(2,1)S(1)} %all_gather.6, bf16[2048,1152]{1,0:T(8,128)(2,1)} %param.13), kind=kOutput, calls=%fused_computation.1 | convolution fusion | flops 150994944 | bytes 4997120 | tf_op jit(solution)/shard_map/dot_general | solution.py:90
  34.8 4.7 %all-to-all-start = ((f32[4,8,1152]{2,1,0:T(8,128)}), f32[4,8,1152]{2,1,0:T(8,128)S(1)}, u32[]{:S(2)}, u32[]{:S(2)}) async-start(f32[4,8,1152]{2,1,0:T(8,128)} %convolution_bitcast_fusion), calls=%async_computation | async-start | bytes 294912 | tf_op jit(solution)/shard_map/all_to_all | solution.py:93
  39.5 9.7 %fusion.21 = f32[32,4096]{1,0:T(8,128)} fusion(bf16[32,2048]{1,0:T(8,128)(2,1)S(1)} %all_gather.6, bf16[2048,4096]{1,0:T(8,128)(2,1)} %param.16), kind=kOutput, calls=%fused_computation.49 | convolution fusion | flops 536870912 | bytes 17432576 | tf_op jit(solution)/shard_map/dot_general | solution.py:92
  49.2 1.0 copy-done.1
  50.2 3.8 %fusion.20 = f32[32,4096]{1,0:T(8,128)} fusion(bf16[32,2048]{1,0:T(8,128)(2,1)S(1)} %all_gather.6, bf16[2048,4096]{1,0:T(8,128)(2,1)S(1)} %copy-done.1), kind=kOutput, calls=%fused_computation.48 | convolution fusion | flops 536870912 | bytes 17432576 | tf_op jit(solution)/shard_map/dot_general | solution.py:91
  54.2 0.6 dynamic-slice
  55.4 0.1 iota_compare_fusion
  55.5 13.8 %all-reduce.6 = bf16[8,4608]{1,0:T(8,128)(2,1)S(1)} all-reduce(f32[8,4608]{1,0:T(8,128)S(1)} %bitcast.29), channel_id=2, replica_groups=mesh['groups'=2,'gx'=4,'gy'=4] {'gy'}, use_global_device_ids=true, to_apply=%region_2.0.clone | all-reduce | flops 36864 | bytes 221184
  69.4 0.1 subtract_convert_fusion.1
  69.6 0.1 fusion.12
  69.7 0.3 fusion.19
  70.0 0.2 fusion.9
  70.2 0.2 fusion.2
  70.5 5.2 %all-gather = bf16[4,2,4096]{2,1,0:T(2,128)(2,1)S(1)} all-gather(bf16[1,2,4096]{2,1,0:T(2,128)(2,1)S(1)} %reshape.97), channel_id=1, replica_groups=mesh['groups'=2,'gx'=4,'gy'=4] {'gy'}, dimensions={0}, use_global_device_ids=true | all-gather | bytes 81920 | tf_op jit(solution)/shard_map/all_gather | solution.py:96
  75.8 11.0 %all_to_all.38 = bf16[8,4,1024]{2,0,1:T(8,128)(2,1)S(1)} all-to-all(bf16[8,4,1024]{2,0,1:T(8,128)(2,1)S(1)} %copy.13), channel_id=1, replica_groups=mesh['groups'=2,'gx'=4,'gy'=4] {'gx'}, dimensions={1} | all-to-all | bytes 131072 | tf_op jit(solution)/shard_map/all_to_all | solution.py:97
  86.8 3.0 %fusion.7 = f32[32,2048]{1,0:T(8,128)S(1)} fusion(bf16[1024,2048]{1,0:T(8,128)(2,1)} %param.14, bf16[8,4,1024]{2,0,1:T(8,128)(2,1)S(1)} %all_to_all.38), kind=kOutput, calls=%fused_computation.14 | convolution fusion | flops 134217728 | bytes 4521984 | tf_op jit(solution)/shard_map/dot_general | solution.py:100
  89.8 2.4 %all-reduce.5.cloned.1.call-done = (f32[32,4096]{1,0:T(8,128)}, f32[32,4096]{1,0:T(8,128)}) async-done(((f32[32,4096]{1,0:T(8,128)}, f32[32,4096]{1,0:T(8,128)}), (f32[32,4096]{1,0:T(8,128)}, f32[32,4096]{1,0:T(8,128)})) %all-reduce.5.cloned.1.call-update) | async-done | bytes 1048592 | tf_op jit(solution)/shard_map/psum | solution.py:98
  92.2 9.8 %fusion = bf16[32,2048]{1,0:T(8,128)(2,1)} fusion(f32[32,2048]{1,0:T(8,128)S(1)} %fusion.7, bf16[4096,2048]{1,0:T(8,128)(2,1)} %param.17, f32[32,4096]{1,0:T(8,128)} %get-tuple-element.5, f32[32,4096]{1,0:T(8,128)} %get-tuple-element.6), kind=kOutput, calls=%fused_computation.2 | convolution fusion | flops 537788416 | bytes 18219008 | tf_op jit(solution)/shard_map/dot_general | solution.py:102
  102.0 19.7 %reduce-scatter.2.cloned.1.call-done = bf16[8,2048]{1,0:T(8,128)(2,1)} async-done(((bf16[32,2048]{1,0:T(8,128)(2,1)}), bf16[8,2048]{1,0:T(8,128)(2,1)}) %reduce-scatter.2.cloned.1.call-update) | async-done | bytes 32784 | tf_op jit(solution)/shard_map/reduce_scatter | solution.py:101
  (30 shorter events, 0.3 us)
Async XLA Ops:
  6.5 63.2 %copy-start = (bf16[2,512,256]{2,1,0:T(8,128)(2,1)S(1)}, bf16[2,512,256]{2,1,0:T(8,128)(2,1)}, u32[]{:S(2)}) copy-start(bf16[2,512,256]{2,1,0:T(8,128)(2,1)} %param.18) | copy-start | bytes 1572868
  34.8 20.7 %all-to-all-start = ((f32[4,8,1152]{2,1,0:T(8,128)}), f32[4,8,1152]{2,1,0:T(8,128)S(1)}, u32[]{:S(2)}, u32[]{:S(2)}) async-start(f32[4,8,1152]{2,1,0:T(8,128)} %convolution_bitcast_fusion), calls=%async_computation | async-start | bytes 294912 | tf_op jit(solution)/shard_map/all_to_all | solution.py:93
  39.5 52.7 %all-reduce.5.cloned.1.call-start = ((), (), s32[]{:S(2)}) async-start(), calls=%async_computation.4 | async-start | bytes 2097152 | tf_op jit(solution)/shard_map/psum | solution.py:98
  39.5 10.7 %copy-start.1 = (bf16[2048,4096]{1,0:T(8,128)(2,1)S(1)}, bf16[2048,4096]{1,0:T(8,128)(2,1)}, u32[]{:S(2)}) copy-start(bf16[2048,4096]{1,0:T(8,128)(2,1)} %param.15) | copy-start | bytes 50331652
  50.2 3.9 %copy-start.4 = (s32[2]{0:T(128)S(1)}, s32[2]{0:T(128)}, u32[]{:S(2)}) copy-start(s32[2]{0:T(128)} %param.21) | copy-start | bytes 28
  50.2 3.9 %copy-start.5 = (u32[32]{0:T(128)S(1)}, u32[32]{0:T(128)}, u32[]{:S(2)}) copy-start(u32[32]{0:T(128)} %constant.23) | copy-start | bytes 388
  50.2 5.2 %copy-start.2 = (s32[2]{0:T(128)S(1)}, s32[2]{0:T(128)}, u32[]{:S(2)}) copy-start(s32[2]{0:T(128)} %param.20) | copy-start | bytes 28
  50.2 20.0 %copy-start.3 = (bf16[2,512,256]{2,1,0:T(8,128)(2,1)S(1)}, bf16[2,512,256]{2,1,0:T(8,128)(2,1)}, u32[]{:S(2)}) copy-start(bf16[2,512,256]{2,1,0:T(8,128)(2,1)} %param.19) | copy-start | bytes 1572868
  54.1 67.6 %reduce-scatter.2.cloned.1.call-start = ((), (), s32[]{:S(2)}) async-start(), calls=%async_computation.3 | async-start | bytes 163840 | tf_op jit(solution)/shard_map/reduce_scatter | solution.py:101
Sparse Core Ops, SparseCore 0:
  54.2 37.9 all-reduce.4
  102.1 19.5 reduce-scatter.1
where the time goes:
time: 129 us
  blocking collectives  52 us (40%)
  matrix products  30.9 us (24%)
  waiting for transfers between devices  22.1 us (17%)
  between operations  14.2 us (11%)
  starting transfers between devices  4.71 us (4%)
  other arithmetic  2.93 us (2%)
  local copies, waits for them, and re-layouts  1.73 us (1%)
    reduce_scatter x1, waiting for transfers between devices, shards(): lax.psum_scatter((block_term + jnp.dot(hidden, down_weight, preferred_ele...  19.7 us
    unnamed x1, blocking collectives  13.8 us
    all_gather x1, blocking collectives, shards(): normed = lax.all_gather(scaled_rows, 'gx', axis=0, tiled=True)  13.6 us
    all_to_all x1, blocking collectives, shards(): lax.all_to_all(grouped, 'gx', split_axis=1, concat_axis=0, tiled=True)  11 us
    dot_general x1, matrix products, shards(): jnp.dot(hidden, down_weight, preferred_element_type=jnp.float32)  9.75 us
    dot_general x1, matrix products, shards(): up_part = jnp.dot(normed, up_weight, preferred_element_type=jnp.float32)  9.72 us
    psum x1, blocking collectives, shards(): totals = lax.psum(jnp.sum(widened * widened, axis=1), 'gy')  8.34 us
    all_gather x1, blocking collectives, shards(): grouped = lax.all_gather(attended, 'gy', axis=0, tiled=True)  5.25 us
  transfers between devices with their start and end apart: 3, of which 2 were waited for; matrix products, arithmetic and copies ran while one was open for 14% of the time, Pallas kernels for 0%

commit v1 on v0

--- a/solution.py
+++ b/solution.py
@@ -1,9 +1,16 @@
+import functools
+
 import jax
 import jax.numpy as jnp
+import numpy as np
 from jax import lax
+from jax.experimental import pallas as pl
+from jax.experimental.pallas import tpu as pltpu
 from jax.sharding import PartitionSpec as P
 
 D = 8192
+LANES = 128
+MESH = pl.DeviceIdType.MESH
 
 
 def angles(token_positions, head_width):
@@ -67,7 +74,7 @@
     return mixed.reshape(row_count, query_width).astype(jnp.bfloat16)
 
 
-def shards(
+def collective_shards(
     residual,
     norm_gain,
     qkv_weight,
@@ -108,6 +115,420 @@
     )
 
 
+def block_kernel(
+    sizes,
+    res_ref, gain_ref, freq_ref, qkv_hbm, out_hbm, gate_hbm, up_hbm, down_hbm, keys_hbm, vals_hbm,
+    len_ref, pos_ref,
+    y_ref,
+    qkv_w, out_w, gate_w, up_w, down_w, keys_v, vals_v,
+    res_send, res_all, ss_all, normed, q_send, q_all, qa, qc, att_send, att_all, att_x,
+    gu_send, gu_all, hid, rs_send, rs_all, head_out,
+    qkv_sem, out_sem, gate_sem, up_sem, down_sem, kv_sem,
+    res_s, res_r, ss_s, ss_r, q_s, q_r, att_s, att_r, gu_s, gu_r, hid_s, hid_r, rs_s, rs_r,
+):
+    nx, ny = sizes["gx"], sizes["gy"]
+    n = nx * ny
+    g, i, j = lax.axis_index("groups"), lax.axis_index("gx"), lax.axis_index("gy")
+    me = i * ny + j
+    rows = res_ref.shape[0]
+    own_rows = q_send.shape[1]
+    half = res_ref.shape[1] // 2
+    chunks, _, cols = gate_w.shape
+    part = cols // ny
+    ychunks, _, ycols = down_w.shape
+    heads = qa.shape[1] - 8
+    f32, bf16 = jnp.float32, jnp.bfloat16
+
+    def peer(d):
+        other = lax.rem(me + d, n)
+        return (g, other // ny, lax.rem(other, ny)), other
+
+    def gate_copy(c):
+        return pltpu.make_async_copy(
+            gate_hbm.at[:, pl.ds(pl.multiple_of(c * cols, cols), cols)], gate_w.at[c], gate_sem.at[c])
+
+    def up_copy(c):
+        return pltpu.make_async_copy(
+            up_hbm.at[:, pl.ds(pl.multiple_of(c * cols, cols), cols)], up_w.at[c], up_sem.at[c])
+
+    def down_copy(c):
+        return pltpu.make_async_copy(
+            down_hbm.at[:, pl.ds(pl.multiple_of(c * ycols, ycols), ycols)], down_w.at[c], down_sem.at[c])
+
+    qkv_copy = pltpu.make_async_copy(qkv_hbm, qkv_w, qkv_sem)
+    out_copy = pltpu.make_async_copy(out_hbm, out_w, out_sem)
+    keys_copy = pltpu.make_async_copy(keys_hbm, keys_v, kv_sem.at[0])
+    vals_copy = pltpu.make_async_copy(vals_hbm, vals_v, kv_sem.at[1])
+
+    qkv_copy.start()
+    keys_copy.start()
+    vals_copy.start()
+
+    def start_gu(c, carry):
+        gate_copy(c).start()
+        up_copy(c).start()
+        return carry
+
+    lax.fori_loop(0, chunks, start_gu, 0)
+    out_copy.start()
+
+    def start_down(c, carry):
+        down_copy(c).start()
+        return carry
+
+    lax.fori_loop(0, ychunks, start_down, 0)
+
+    barrier = pltpu.get_barrier_semaphore()
+
+    def greet(d, carry):
+        target, _ = peer(d)
+        pl.semaphore_signal(barrier, inc=1, device_id=target, device_id_type=MESH)
+        return carry
+
+    lax.fori_loop(1, n, greet, 0)
+
+    own = res_ref[...].astype(f32)
+    packed = jnp.concatenate([own[:, :half], own[:, half:]], axis=0).astype(bf16)
+    res_send[...] = packed
+    res_all[i] = packed
+    squares = jnp.sum(own * own, axis=1, keepdims=True)
+    diagonal = lax.broadcasted_iota(jnp.int32, (rows, LANES), 0) == lax.broadcasted_iota(
+        jnp.int32, (rows, LANES), 1)
+    in_lanes = jnp.sum(jnp.where(diagonal, squares, 0.0), axis=0, keepdims=True)
+    ss_all[me] = in_lanes
+
+    pl.semaphore_wait(barrier, n - 1)
+
+    def send_res(d, carry):
+        to = lax.rem(i + d, nx)
+        pltpu.make_async_remote_copy(
+            src_ref=res_send, dst_ref=res_all.at[i], send_sem=res_s, recv_sem=res_r,
+            device_id=(g, to, j), device_id_type=MESH).start()
+        return carry
+
+    def send_ss(d, carry):
+        target, _ = peer(d)
+        pltpu.make_async_remote_copy(
+            src_ref=ss_all.at[me], dst_ref=ss_all.at[me], send_sem=ss_s, recv_sem=ss_r,
+            device_id=target, device_id_type=MESH).start()
+        return carry
+
+    lax.fori_loop(1, nx, send_res, 0)
+    lax.fori_loop(1, n, send_ss, 0)
+
+    def drain(ref, sem):
+        pltpu.make_async_copy(ref, ref, sem).wait()
+
+    drain(ss_all.at[pl.ds(0, n - 1)], ss_r)
+    drain(res_all.at[pl.ds(0, nx - 1)], res_r)
+
+    gain = gain_ref[...].astype(f32)
+    blocks = []
+    for block in range(nx):
+        lanes = ss_all[block * ny]
+        for other in range(1, ny):
+            lanes = lanes + ss_all[block * ny + other]
+        total = jnp.sum(jnp.where(diagonal, lanes, 0.0), axis=1, keepdims=True)
+        scale = lax.rsqrt(total / D + 1e-06)
+        wide = res_all[block].astype(f32)
+        wide = jnp.concatenate([wide[:rows], wide[rows:]], axis=1)
+        blocks.append(wide * scale * gain)
+    normed[...] = jnp.concatenate(blocks, axis=0).astype(bf16)
+
+    qkv_copy.wait()
+    qkv_part = jnp.dot(normed[...], qkv_w[...], preferred_element_type=f32)
+    for to in range(n):
+        q_send[to] = qkv_part[to * own_rows:(to + 1) * own_rows, :]
+    q_all[me] = q_send[me]
+
+    def send_q(d, carry):
+        target, other = peer(d)
+        pltpu.make_async_remote_copy(
+            src_ref=q_send.at[other], dst_ref=q_all.at[me], send_sem=q_s, recv_sem=q_r,
+            device_id=target, device_id_type=MESH).start()
+        return carry
+
+    lax.fori_loop(1, n, send_q, 0)
+
+    def gu_step(c, carry):
+        gate_copy(c).wait()
+        gate = jnp.dot(normed[...], gate_w[c], preferred_element_type=f32).astype(bf16)
+        for to in range(ny):
+            gu_send[c, to, 0] = gate[:, to * part:(to + 1) * part]
+        up_copy(c).wait()
+        up = jnp.dot(normed[...], up_w[c], preferred_element_type=f32).astype(bf16)
+        for to in range(ny):
+            gu_send[c, to, 1] = up[:, to * part:(to + 1) * part]
+        gu_all[c, j] = gu_send[c, j]
+
+        def send_gu(d, inner):
+            to = lax.rem(j + d, ny)
+            pltpu.make_async_remote_copy(
+                src_ref=gu_send.at[c, to], dst_ref=gu_all.at[c, j], send_sem=gu_s,
+                recv_sem=gu_r.at[c], device_id=(g, i, to), device_id_type=MESH).start()
+            return inner
+
+        lax.fori_loop(1, ny, send_gu, 0)
+        return carry
+
+    def hid_step(c, carry):
+        drain(gu_all.at[c, pl.ds(0, ny - 1)], gu_r.at[c])
+        gate = gu_all[c, 0, 0].astype(f32)
+        up = gu_all[c, 0, 1].astype(f32)
+        for other in range(1, ny):
+            gate = gate + gu_all[c, other, 0].astype(f32)
+            up = up + gu_all[c, other, 1].astype(f32)
+        here = hid.at[:, pl.ds(pl.multiple_of(c * cols + j * part, part), part)]
+        here[...] = (gate / (1.0 + jnp.exp(-gate)) * up).astype(bf16)
+
+        def send_hid(d, inner):
+            to = lax.rem(j + d, ny)
+            pltpu.make_async_remote_copy(
+                src_ref=here, dst_ref=here, send_sem=hid_s, recv_sem=hid_r,
+                device_id=(g, i, to), device_id_type=MESH).start()
+            return inner
+
+        lax.fori_loop(1, ny, send_hid, 0)
+        return carry
+
+    early = sizes["early"]
+    lag = sizes["lag"]
+    lax.fori_loop(0, early, gu_step, 0)
+
+    drain(q_all.at[pl.ds(0, n - 1)], q_r)
+    per = q_all.shape[2] // LANES
+    for block in range(nx):
+        summed = q_all[block * ny]
+        for other in range(1, ny):
+            summed = summed + q_all[block * ny + other]
+        summed = summed.astype(bf16).astype(f32)
+        for at in range(per):
+            index = block * per + at
+            into = qa if index % 2 == 0 else qc
+            for r in range(own_rows):
+                into[r, index // 2:index // 2 + 1, :] = summed[r:r + 1, at * LANES:(at + 1) * LANES]
+    keys_copy.wait()
+    vals_copy.wait()
+    context = keys_v.shape[1]
+    score_scale = keys_v.shape[2] ** (-0.5)
+    per_block = heads // nx
+    for r in range(own_rows):
+        turn = freq_ref[...] * pos_ref[r].astype(f32)
+        cosine, sine = jnp.cos(turn), jnp.sin(turn)
+
+        def rotated(a, c):
+            return jnp.concatenate([a * cosine - c * sine, a * sine + c * cosine], axis=1).astype(bf16)
+
+        queries = rotated(qa[r, 0:heads, :], qc[r, 0:heads, :])
+        new_key = rotated(qa[r, heads:heads + 1, :], qc[r, heads:heads + 1, :])
+        new_value = jnp.concatenate(
+            [qa[r, heads + 1:heads + 2, :], qc[r, heads + 1:heads + 2, :]], axis=1)
+        scores = lax.dot_general(
+            queries, keys_v[r], (((1,), (1,)), ((), ())), preferred_element_type=f32) * score_scale
+        visible = lax.broadcasted_iota(jnp.int32, (heads, context), 1) < len_ref[r]
+        scores = jnp.where(visible, scores, -jnp.inf)
+        own_score = jnp.sum(
+            queries.astype(f32) * new_key.astype(f32), axis=1, keepdims=True) * score_scale
+        top = jnp.maximum(jnp.max(scores, axis=1, keepdims=True), own_score)
+        shifted = jnp.exp(scores - top)
+        own_shifted = jnp.exp(own_score - top)
+        total = jnp.sum(shifted, axis=1, keepdims=True) + own_shifted
+        weights = (shifted / total).astype(bf16)
+        own_weight = (own_shifted / total).astype(bf16).astype(f32)
+        mixed = jnp.dot(weights, vals_v[r], preferred_element_type=f32) + own_weight * new_value
+        mixed = mixed.astype(bf16).astype(f32)
+        width = mixed.shape[1]
+        for h in range(heads):
+            at = h % per_block
+            att_send[h // per_block, r:r + 1, at * width:(at + 1) * width] = mixed[h:h + 1, :]
+    att_all[me] = att_send[i]
+
+    def send_att(d, carry):
+        target, other = peer(d)
+        pltpu.make_async_remote_copy(
+            src_ref=att_send.at[other // ny], dst_ref=att_all.at[me], send_sem=att_s,
+            recv_sem=att_r, device_id=target, device_id_type=MESH).start()
+        return carry
+
+    lax.fori_loop(1, n, send_att, 0)
+
+    def both(c, carry):
+        gu_step(c, 0)
+        hid_step(c - lag, 0)
+        return carry
+
+    lax.fori_loop(early, lag, gu_step, 0)
+    lax.fori_loop(max(early, lag), chunks, both, 0)
+    lax.fori_loop(max(chunks - lag, 0), chunks, hid_step, 0)
+
+    drain(att_all.at[pl.ds(0, n - 1)], att_r)
+    for source in range(n):
+        att_x[source * own_rows:(source + 1) * own_rows, :] = att_all[source]
+    out_copy.wait()
+    attended = att_x[...].astype(bf16)
+
+    def out_step(c, carry):
+        at = pl.ds(pl.multiple_of(c * ycols, ycols), ycols)
+        head_out[c] = jnp.dot(attended, out_w[:, at], preferred_element_type=f32)
+        return carry
+
+    lax.fori_loop(0, ychunks, out_step, 0)
+
+    drain(hid.at[:, pl.ds(0, chunks * part * (ny - 1))], hid_r)
+
+    def down_step(c, carry):
+        down_copy(c).wait()
+        term = head_out[c] + jnp.dot(hid[...], down_w[c], preferred_element_type=f32)
+        for to in range(nx):
+            mine = term[to * rows:(to + 1) * rows]
+            rs_send[c, to] = jnp.concatenate(
+                [mine[:, :ycols // 2], mine[:, ycols // 2:]], axis=0).astype(bf16)
+        rs_all[c, i] = rs_send[c, i]
+
+        def send_rs(d, inner):
+            to = lax.rem(i + d, nx)
+            pltpu.make_async_remote_copy(
+                src_ref=rs_send.at[c, to], dst_ref=rs_all.at[c, i], send_sem=rs_s,
+                recv_sem=rs_r.at[c], device_id=(g, to, j), device_id_type=MESH).start()
+            return inner
+
+        lax.fori_loop(1, nx, send_rs, 0)
+        return carry
+
+    lax.fori_loop(0, ychunks, down_step, 0)
+
+    for c in range(ychunks):
+        drain(rs_all.at[c, pl.ds(0, nx - 1)], rs_r.at[c])
+        total = rs_all[c, 0].astype(f32)
+        for other in range(1, nx):
+            total = total + rs_all[c, other].astype(f32)
+        y_ref[:, c * ycols:(c + 1) * ycols] = jnp.concatenate(
+            [total[:rows], total[rows:]], axis=1).astype(bf16)
+
+    def drain_res(d, carry):
+        drain(res_send, res_s)
+        return carry
+
+    lax.fori_loop(1, nx, drain_res, 0)
+    drain(ss_all.at[pl.ds(0, n - 1)], ss_s)
+    drain(q_all.at[pl.ds(0, n - 1)], q_s)
+    drain(att_all.at[pl.ds(0, n - 1)], att_s)
+    drain(gu_all.at[:, pl.ds(0, ny - 1)], gu_s)
+    drain(hid.at[:, pl.ds(0, chunks * part * (ny - 1))], hid_s)
+    drain(rs_all.at[:, pl.ds(0, nx - 1)], rs_s)
+
+
+def kernel_shards(
+    nx,
+    ny,
+    residual,
+    norm_gain,
+    qkv_weight,
+    out_weight,
+    gate_weight,
+    up_weight,
+    down_weight,
+    cache_keys,
+    cache_values,
+    lengths,
+    positions,
+):
+    n = nx * ny
+    rows, features = residual.shape
+    own_rows, context, width = cache_keys.shape
+    batch = rows * nx
+    qkv_cols = qkv_weight.shape[1]
+    heads = out_weight.shape[0] * nx // width
+    units = gate_weight.shape[1]
+    cols = LANES * ny
+    chunks = units // cols
+    ycols = 512
+    ychunks = features // ycols
+    half = width // 2
+    frequency = np.exp(np.arange(half) * (-2.0 * np.log(10000.0) / width)).astype(np.float32)
+    f32, bf16 = jnp.float32, jnp.bfloat16
+    sem = pltpu.SemaphoreType.DMA
+    vmem = pl.BlockSpec(memory_space=pltpu.VMEM)
+    smem = pl.BlockSpec(memory_space=pltpu.SMEM)
+    hbm = pl.BlockSpec(memory_space=pl.ANY)
+    sizes = {"gx": nx, "gy": ny, "early": 2, "lag": 4}
+    return pl.pallas_call(
+        functools.partial(block_kernel, sizes),
+        out_shape=jax.ShapeDtypeStruct((rows, features), bf16),
+        in_specs=[vmem, vmem, vmem] + [hbm] * 7 + [smem, smem],
+        out_specs=vmem,
+        scratch_shapes=[
+            pltpu.VMEM((features, qkv_cols), bf16),
+            pltpu.VMEM(out_weight.shape, bf16),
+            pltpu.VMEM((chunks, features, cols), bf16),
+            pltpu.VMEM((chunks, features, cols), bf16),
+            pltpu.VMEM((ychunks, units, ycols), bf16),
+            pltpu.VMEM(cache_keys.shape, bf16),
+            pltpu.VMEM(cache_values.shape, bf16),
+            pltpu.VMEM((2 * rows, features // 2), bf16),
+            pltpu.VMEM((nx, 2 * rows, features // 2), bf16),
+            pltpu.VMEM((n, 1, LANES), f32),
+            pltpu.VMEM((batch, features), bf16),
+            pltpu.VMEM((n, own_rows, qkv_cols), f32),
+            pltpu.VMEM((n, own_rows, qkv_cols), f32),
+            pltpu.VMEM((own_rows, heads + 8, half), f32),
+            pltpu.VMEM((own_rows, heads + 8, half), f32),
+            pltpu.VMEM((nx, own_rows, heads // nx * width), f32),
+            pltpu.VMEM((n, own_rows, heads // nx * width), f32),
+            pltpu.VMEM((batch, heads // nx * width), f32),
+            pltpu.VMEM((chunks, ny, 2, batch, LANES), bf16),
+            pltpu.VMEM((chunks, ny, 2, batch, LANES), bf16),
+            pltpu.VMEM((batch, units), bf16),
+            pltpu.VMEM((ychunks, nx, 2 * rows, ycols // 2), bf16),
+            pltpu.VMEM((ychunks, nx, 2 * rows, ycols // 2), bf16),
+            pltpu.VMEM((ychunks, batch, ycols), f32),
+            sem, sem, sem((chunks,)), sem((chunks,)), sem((ychunks,)), sem((2,)),
+            sem, sem, sem, sem, sem, sem, sem, sem,
+            sem, sem((chunks,)), sem, sem, sem, sem((ychunks,)),
+        ],
+        compiler_params=pltpu.CompilerParams(
+            collective_id=0, has_side_effects=True, vmem_limit_bytes=64 * 1024 * 1024 - 65536),
+    )(
+        residual,
+        norm_gain.reshape(1, features),
+        jnp.asarray(frequency).reshape(1, half),
+        qkv_weight,
+        out_weight,
+        gate_weight,
+        up_weight,
+        down_weight,
+        cache_keys,
+        cache_values,
+        lengths,
+        positions,
+    )
+
+
+def fits_kernel(nx, ny, residual, qkv_weight, out_weight, gate_weight, cache_keys):
+    rows, features = residual.shape
+    own_rows, _, width = cache_keys.shape
+    units = gate_weight.shape[1]
+    held = features * (qkv_weight.shape[1] + 3 * units) + out_weight.size + 2 * cache_keys.size
+    return (
+        rows == 8
+        and rows == own_rows * ny
+        and width == 2 * LANES
+        and qkv_weight.shape[1] % LANES == 0
+        and out_weight.shape[0] % width == 0
+        and units % (LANES * ny) == 0
+        and units // (LANES * ny) >= 4
+        and features % 512 == 0
+        and 2 * held <= 58 * 1024 * 1024
+    )
+
+
+def shards(nx, ny, *operands):
+    residual, _, qkv_weight, out_weight, gate_weight, _, _, cache_keys = operands[:8]
+    if fits_kernel(nx, ny, residual, qkv_weight, out_weight, gate_weight, cache_keys):
+        return kernel_shards(nx, ny, *operands)
+    return collective_shards(*operands)
+
+
 def solution(mesh):
     in_specs = (
         P(("groups", "gx"), "gy"),
@@ -123,4 +544,5 @@
         P(("groups", "gx", "gy")),
     )
     out_specs = P(("groups", "gx"), "gy")
-    return jax.shard_map(shards, mesh=mesh, in_specs=in_specs, out_specs=out_specs, check_vma=False)
+    body = functools.partial(shards, mesh.shape["gx"], mesh.shape["gy"])
+    return jax.shard_map(body, mesh=mesh, in_specs=in_specs, out_specs=out_specs, check_vma=False)

time: 129 us -> 42 us (0.33)
  blocking collectives: 52 us -> 0 us
  Pallas kernels: 0 us -> 39.1 us
  matrix products: 30.9 us -> 0 us
  waiting for transfers between devices: 22.1 us -> 0 us
  between operations: 14.2 us -> 0.01 us
  starting transfers between devices: 4.71 us -> 0 us
  other arithmetic: 2.93 us -> 0 us
    pallas_call x0 -> x1, Pallas kernels: none -> 39.1 us  [kernel_shards(): pl.pallas_call(functools.partial(block_kernel, sizes), out_shape=jax.Shap...]
    dot_general x8 -> x0, matrix products: 30.9 us -> none  [the longest x1 9.75 us: shards(): jnp.dot(hidden, down_weight, preferred_element_type=jnp.float32)]
    reduce_scatter x1 -> x0, waiting for transfers between devices: 19.7 us -> none  [shards(): lax.psum_scatter((block_term + jnp.dot(hidden, down_weight, preferred_ele...]
    all_gather x2 -> x0, blocking collectives: 18.8 us -> none  [the longest x1 13.6 us: shards(): normed = lax.all_gather(scaled_rows, 'gx', axis=0, tiled=True)]
    unnamed x1 -> x0, blocking collectives: 13.8 us -> none
    all_to_all x1 -> x0, blocking collectives: 11 us -> none  [shards(): lax.all_to_all(grouped, 'gx', split_axis=1, concat_axis=0, tiled=True)]
    psum x1 -> x0, blocking collectives: 8.34 us -> none  [shards(): totals = lax.psum(jnp.sum(widened * widened, axis=1), 'gy')]
    all_to_all x1 -> x0, starting transfers between devices: 4.66 us -> none  [shards(): lax.all_to_all(qkv_part, 'gx', split_axis=0, concat_axis=1, tiled=True)]
  transfers between devices with their start and end apart: 3 -> 0, of which waited for: 2 -> 0; matrix products, arithmetic and copies ran while one was open for 14% -> 0% of each run, Pallas kernels for 0% -> 0%
where the time goes in v1:
time: 42 us; the launch traced here: 41.7 us
  Pallas kernels  39.1 us (93%)
  local copies, waits for them, and re-layouts  2.67 us (6%)
    pallas_call x1, Pallas kernels, kernel_shards(): pl.pallas_call(functools.partial(block_kernel, sizes), out_shape=jax.Shap...  39.1 us
    unnamed x1, local copies, waits for them, and re-layouts  1.38 us
    reshape x1, local copies, waits for them, and re-layouts, kernel_shards(): norm_gain.reshape(1, features)  1.29 us

profile of v1, /device:TPU:0, one launch (start us, length us, event | category | flops | bytes accessed | tf_op | source)
XLA Modules:
  0.0 41.7 jit_solution(14041629231621759020)
XLA Ops:
  0.0 1.3 %reshape.6.gain_ref = bf16[1,2048]{1,0:T(2,128)(2,1)} reshape(bf16[2048]{0:T(1024)(128)(2,1)} %param.13) | data formatting | bytes 8192 | tf_op jit(solution)/shard_map/reshape | solution.py:493
  1.3 39.1 %shard_map.118 = bf16[8,2048]{1,0:T(8,128)(2,1)} custom-call(bf16[8,2048]{1,0:T(8,128)(2,1)} %res_ref.1, bf16[1,2048]{1,0:T(2,128)(2,1)} %reshape.6.gain_ref, f32[1,128]{1,0:T(1,128)} %constant.7.freq_ref, bf16[2048,1152]{1,0:T(8,128)(2,1)} %qkv_hbm.1, bf16[1024,2048]{1,0:T(8,128)(2,1)} %out_hbm.1, bf16[2048,4096]{1,0:T(8,128)(2,1)} %gate_hbm.1, ...), custom_call_target="tpu_custom_call" | custom-call | tf_op jit(solution)/shard_map/pallas_call | solution.py:455
  40.4 1.4 %copy.14 = bf16[8,2048]{1,0:T(8,128)(2,1)} copy(bf16[8,2048]{1,0:T(8,128)(2,1)} %shard_map.118) | data formatting | bytes 65536

commit v2 on v1

--- a/solution.py
+++ b/solution.py
@@ -222,7 +222,7 @@
     drain(ss_all.at[pl.ds(0, n - 1)], ss_r)
     drain(res_all.at[pl.ds(0, nx - 1)], res_r)
 
-    gain = gain_ref[...].astype(f32)
+    gain = gain_ref[...].astype(f32).reshape(1, 2 * half)
     blocks = []
     for block in range(nx):
         lanes = ss_all[block * ny]
@@ -293,7 +293,18 @@
 
     early = sizes["early"]
     lag = sizes["lag"]
-    lax.fori_loop(0, early, gu_step, 0)
+
+    def both(c, carry):
+        gu_step(c, 0)
+        hid_step(c - lag, 0)
+        return carry
+
+    def run(first, end):
+        middle = min(max(first, lag), end)
+        lax.fori_loop(first, middle, gu_step, 0)
+        lax.fori_loop(middle, end, both, 0)
+
+    run(0, early)
 
     drain(q_all.at[pl.ds(0, n - 1)], q_r)
     per = q_all.shape[2] // LANES
@@ -352,14 +363,8 @@
 
     lax.fori_loop(1, n, send_att, 0)
 
-    def both(c, carry):
-        gu_step(c, 0)
-        hid_step(c - lag, 0)
-        return carry
-
-    lax.fori_loop(early, lag, gu_step, 0)
-    lax.fori_loop(max(early, lag), chunks, both, 0)
-    lax.fori_loop(max(chunks - lag, 0), chunks, hid_step, 0)
+    run(early, chunks)
+    lax.fori_loop(chunks - lag, chunks, hid_step, 0)
 
     drain(att_all.at[pl.ds(0, n - 1)], att_r)
     for source in range(n):
@@ -451,7 +456,7 @@
     vmem = pl.BlockSpec(memory_space=pltpu.VMEM)
     smem = pl.BlockSpec(memory_space=pltpu.SMEM)
     hbm = pl.BlockSpec(memory_space=pl.ANY)
-    sizes = {"gx": nx, "gy": ny, "early": 2, "lag": 4}
+    sizes = {"gx": nx, "gy": ny, "early": min(7, chunks), "lag": min(6, chunks)}
     return pl.pallas_call(
         functools.partial(block_kernel, sizes),
         out_shape=jax.ShapeDtypeStruct((rows, features), bf16),
@@ -490,7 +495,7 @@
             collective_id=0, has_side_effects=True, vmem_limit_bytes=64 * 1024 * 1024 - 65536),
     )(
         residual,
-        norm_gain.reshape(1, features),
+        norm_gain,
         jnp.asarray(frequency).reshape(1, half),
         qkv_weight,
         out_weight,
@@ -516,7 +521,7 @@
         and qkv_weight.shape[1] % LANES == 0
         and out_weight.shape[0] % width == 0
         and units % (LANES * ny) == 0
-        and units // (LANES * ny) >= 4
+        and units // (LANES * ny) >= 6
         and features % 512 == 0
         and 2 * held <= 58 * 1024 * 1024
     )

time: 42 us -> 37.6 us (0.90)
  Pallas kernels: 39.1 us -> 36 us
  local copies, waits for them, and re-layouts: 2.67 us -> 1.38 us
    pallas_call x1, Pallas kernels: 39.1 us -> 36 us  [kernel_shards(): pl.pallas_call(functools.partial(block_kernel, sizes), out_shape=jax.Shap...]
    reshape x1 -> x0, local copies, waits for them, and re-layouts: 1.29 us -> none  [kernel_shards(): norm_gain.reshape(1, features)]
where the time goes in v2:
time: 37.6 us; the launch traced here: 37.4 us
  Pallas kernels  36 us (96%)
  local copies, waits for them, and re-layouts  1.38 us (4%)
    pallas_call x1, Pallas kernels, kernel_shards(): pl.pallas_call(functools.partial(block_kernel, sizes), out_shape=jax.Shap...  36 us
    unnamed x1, local copies, waits for them, and re-layouts  1.38 us

profile of v2, /device:TPU:0, one launch (start us, length us, event | category | flops | bytes accessed | tf_op | source)
XLA Modules:
  0.0 37.4 jit_solution(9436562445434178753)
XLA Ops:
  0.0 36.0 %shard_map.118 = bf16[8,2048]{1,0:T(8,128)(2,1)} custom-call(bf16[8,2048]{1,0:T(8,128)(2,1)} %res_ref.1, bf16[2048]{0:T(1024)(128)(2,1)} %gain_ref.1, f32[1,128]{1,0:T(1,128)} %constant.7.freq_ref, bf16[2048,1152]{1,0:T(8,128)(2,1)} %qkv_hbm.1, bf16[1024,2048]{1,0:T(8,128)(2,1)} %out_hbm.1, bf16[2048,4096]{1,0:T(8,128)(2,1)} %gate_hbm.1, ...), custom_call_target="tpu_custom_call" | custom-call | tf_op jit(solution)/shard_map/pallas_call | solution.py:460
  36.0 1.4 %copy.14 = bf16[8,2048]{1,0:T(8,128)(2,1)} copy(bf16[8,2048]{1,0:T(8,128)(2,1)} %shard_map.118) | data formatting | bytes 65536

commit v3 on v2

--- a/solution.py
+++ b/solution.py
@@ -447,7 +447,7 @@
     units = gate_weight.shape[1]
     cols = LANES * ny
     chunks = units // cols
-    ycols = 512
+    ycols = 1024
     ychunks = features // ycols
     half = width // 2
     frequency = np.exp(np.arange(half) * (-2.0 * np.log(10000.0) / width)).astype(np.float32)

time: 37.6 us -> 37.5 us (level)
  no operation moved by 1% of the time
where the time goes in v3:
time: 37.5 us; the launch traced here: 37.2 us
  Pallas kernels  35.8 us (95%)
  local copies, waits for them, and re-layouts  1.38 us (4%)
    pallas_call x1, Pallas kernels, kernel_shards(): pl.pallas_call(functools.partial(block_kernel, sizes), out_shape=jax.Shap...  35.8 us
    unnamed x1, local copies, waits for them, and re-layouts  1.38 us

profile of v3, /device:TPU:0, one launch (start us, length us, event | category | flops | bytes accessed | tf_op | source)
XLA Modules:
  0.0 37.2 jit_solution(4503179546599542717)
XLA Ops:
  0.0 35.8 %shard_map.118 = bf16[8,2048]{1,0:T(8,128)(2,1)} custom-call(bf16[8,2048]{1,0:T(8,128)(2,1)} %res_ref.1, bf16[2048]{0:T(1024)(128)(2,1)} %gain_ref.1, f32[1,128]{1,0:T(1,128)} %constant.7.freq_ref, bf16[2048,1152]{1,0:T(8,128)(2,1)} %qkv_hbm.1, bf16[1024,2048]{1,0:T(8,128)(2,1)} %out_hbm.1, bf16[2048,4096]{1,0:T(8,128)(2,1)} %gate_hbm.1, ...), custom_call_target="tpu_custom_call" | custom-call | tf_op jit(solution)/shard_map/pallas_call | solution.py:460
  35.8 1.4 %copy.14 = bf16[8,2048]{1,0:T(8,128)(2,1)} copy(bf16[8,2048]{1,0:T(8,128)(2,1)} %shard_map.118) | data formatting | bytes 65536
